TPU v7x, 32 devices: a whole 2x2x4 slice. The times are simulated.
32 devices in a mesh: seq: 8 (over z, y), wt: 4 (over x, core).
Axes of the slice: x: 2, y: 2, z: 4, core: 2. Of those that a mesh axis runs over, the one named last changes fastest.
Arguments:
- activations: bfloat16 [16384, 1536], P('seq', 'wt'), may hold values from -6 to 6
- first_norm_scale: float32 [1536], P('wt'), may hold values from 0.1 to 1.9
- first_norm_shift: float32 [1536], P('wt'), may hold values from -0.5 to 0.5
- first_kernel_weight: bfloat16 [3, 1536, 1536], P(None, 'seq', 'wt'), may hold values from -0.09375 to 0.09375
- second_norm_scale: float32 [1536], P('wt'), may hold values from 0.1 to 1.9
- second_norm_shift: float32 [1536], P('wt'), may hold values from -0.5 to 0.5
- second_kernel_weight: bfloat16 [3, 1536, 1536], P(None, 'seq', 'wt'), may hold values from -0.09375 to 0.09375
Outputs:
- tower_out: bfloat16 [16384, 1536], P('seq', 'wt')
All inputs are finite; a program needn't handle non-finite values.
Results may differ from a plain program's by a relative error of at most 0.008.
Values may be sent and summed in bfloat16 or wider, within the bound.
A program may use at most 64 MiB of HBM per device.

v0:
```python
import jax
import jax.numpy as jnp
from jax import lax
from jax.sharding import PartitionSpec as P

DILATION_FIRST = 256
DILATION_SECOND = 512


def padded(cells, sides, width):
    for axis, dim in sides:
        count = lax.axis_size(axis)
        ends = count - 1
        head = lax.slice_in_dim(cells, 0, width, axis=dim)
        tail = lax.slice_in_dim(cells, cells.shape[dim] - width, cells.shape[dim], axis=dim)
        cells = jnp.concatenate(
            [
                lax.ppermute(tail, axis, [(i, (i + 1) % count) for i in range(ends)]),
                cells,
                lax.ppermute(head, axis, [((i + 1) % count, i) for i in range(ends)]),
            ],
            axis=dim,
        )
    return cells


def normed(state, scale, shift):
    value = state.astype(jnp.float32) * scale[None, :] + shift[None, :]
    return jax.nn.gelu(value, approximate=True).astype(jnp.bfloat16)


def widen(hidden, reach):
    narrow = padded(hidden, (("seq", 0),), reach)
    return lax.all_gather(narrow, "wt", axis=1, tiled=True)


def conv_layer(state, scale, shift, weight, reach):
    hidden = normed(state, scale, shift)
    extended = widen(hidden, reach)
    count = state.shape[0]
    kernel = lax.all_gather(weight, "seq", axis=1, tiled=True)
    total = jnp.zeros((count, kernel.shape[2]), jnp.float32)
    for tap in range(3):
        total = total + jnp.dot(
            extended[tap * reach : tap * reach + count],
            kernel[tap],
            preferred_element_type=jnp.float32,
        )
    return (state.astype(jnp.float32) + total).astype(jnp.bfloat16)


def shards(
    activations,
    first_norm_scale,
    first_norm_shift,
    first_kernel_weight,
    second_norm_scale,
    second_norm_shift,
    second_kernel_weight,
):
    first_conv_layer = conv_layer(
        activations, first_norm_scale, first_norm_shift, first_kernel_weight, DILATION_FIRST
    )
    return conv_layer(
        first_conv_layer,
        second_norm_scale,
        second_norm_shift,
        second_kernel_weight,
        DILATION_SECOND,
    )


def solution(mesh):
    placed = (
        P("seq", "wt"),
        P("wt"),
        P("wt"),
        P(None, "seq", "wt"),
        P("wt"),
        P("wt"),
        P(None, "seq", "wt"),
    )
    return jax.shard_map(
        shards, mesh=mesh, in_specs=placed, out_specs=P("seq", "wt"), check_vma=False
    )
```

profile of v0, /device:TPU:0, one launch (start us, length us, event | category | flops | bytes accessed | tf_op | source)
XLA Modules:
  0.0 291.0 jit_solution(8754537896223465314)
XLA Ops:
  6.5 0.0 all-gather.7.cloned.1.call-start
  6.5 0.7 all-gather.7.cloned.1.call-update
  7.3 0.0 all-gather.5.cloned.1.call-start
  7.3 2.7 fusion.15
  10.1 4.9 %collective-permute-start = (bf16[256,384]{1,0:T(8,128)(2,1)S(1)}, bf16[256,384]{1,0:T(8,128)(2,1)S(1)}, u32[]{:S(2)}, u32[]{:S(2)}) collective-permute-start(bf16[256,384]{1,0:T(8,128)(2,1)S(1)} %get-tuple-element.7), channel_id=1, source_target_pairs={{0,4},{4,8},{8,12},{12,16},{16,20},{20,24},{24,28},{1,5},{5,9},{9,... | collective-permute-start | bytes 589832 | tf_op jit(solution)/shard_map/ppermute | solution.py:18
  15.0 1.3 collective-permute-start.1
  16.3 2.9 collective-permute-done
  19.2 4.2 %collective-permute-done.1 = bf16[256,384]{1,0:T(8,128)(2,1)S(1)} collective-permute-done((bf16[256,384]{1,0:T(8,128)(2,1)S(1)}, bf16[256,384]{1,0:T(8,128)(2,1)S(1)}, u32[]{:S(2)}, u32[]{:S(2)}) %collective-permute-start.1) | collective-permute-done | bytes 196640 | tf_op jit(solution)/shard_map/ppermute | solution.py:20
  23.4 1.5 pad_maximum_fusion.1
  24.8 0.0 all-gather.5.cloned.1.call-update
  24.8 0.0 all-gather.11.cloned.1.call-start
  24.9 0.7 all-gather.11.cloned.1.call-update
  25.6 0.0 all-gather.9.cloned.1.call-start
  25.6 52.4 %all-gather.7.cloned.1.call-done = bf16[3,1536,384]{2,1,0:T(8,128)(2,1)} async-done(((bf16[3,192,384]{2,1,0:T(8,128)(2,1)}), bf16[3,1536,384]{2,1,0:T(8,128)(2,1)}) %all-gather.7.cloned.1.call-update) | async-done | bytes 3538960 | tf_op jit(solution)/shard_map/all_gather | solution.py:41
  78.0 0.0 copy-start.4
  78.0 55.3 %all-gather.5.cloned.1.call-done = bf16[2560,1536]{1,0:T(8,128)(2,1)} async-done(((bf16[2560,384]{1,0:T(8,128)(2,1)}), bf16[2560,1536]{1,0:T(8,128)(2,1)}) %all-gather.5.cloned.1.call-update) | async-done | bytes 7864336 | tf_op jit(solution)/shard_map/all_gather | solution.py:34
  133.3 0.0 copy-start.2
  133.3 6.0 %fusion.8 = f32[2048,384]{1,0:T(8,128)S(1)} fusion(bf16[2560,1536]{1,0:T(8,128)(2,1)} %all-gather.5.cloned.1.call-done, bf16[3,1536,384]{2,1,0:T(8,128)(2,1)} %all-gather.7.cloned.1.call-done), kind=kOutput, calls=%fused_computation.8 | convolution fusion | flops 2415919104 | bytes 10616832 | tf_op jit(solution)/shard_map/dot_general | solution.py:44
  139.3 0.0 copy-done.4
  139.3 0.0 copy-done.2
  139.3 0.0 copy-start
  139.3 0.0 copy-start.5
  139.3 0.0 copy-start.6
  139.3 3.4 %fusion.10 = f32[2048,384]{1,0:T(8,128)S(1)} fusion(bf16[2560,1536]{1,0:T(8,128)(2,1)S(1)} %copy-done.2, bf16[3,1536,384]{2,1,0:T(8,128)(2,1)S(1)} %copy-done.4), kind=kOutput, calls=%fused_computation.10 | convolution fusion | flops 2415919104 | bytes 10616832 | tf_op jit(solution)/shard_map/dot_general | solution.py:44
  142.8 0.0 copy-done
  142.8 0.0 copy-done.5
  142.8 0.0 copy-done.6
  142.8 5.7 %fusion.24 = (bf16[2048,384]{1,0:T(8,128)(2,1)S(1)}, bf16[2048,384]{1,0:T(8,128)(2,1)}) fusion(f32[384]{0:T(512)S(1)} %copy-done.5, f32[384]{0:T(512)S(1)} %copy-done.6, bf16[3,1536,384]{2,1,0:T(8,128)(2,1)S(1)} %copy-done.4, bf16[2560,1536]{1,0:T(8,128)(2,1)S(1)} %copy-done.2, f32[2048,384]{1,0:T(8,128)S(1)} %fusion.10, f32[2048,384]{1,0:T(8,128)S(1)} %fusion.8, ...), kind=kOutput, calls=%fused_computation.30 | convolution fusion | flops 2429288448 | bytes 18485248 | tf_op jit(solution)/shard_map/dot_general | solution.py:44
  148.6 0.1 fusion.36
  148.6 3.4 %collective-permute-start.2 = (bf16[512,384]{1,0:T(8,128)(2,1)S(1)}, bf16[512,384]{1,0:T(8,128)(2,1)S(1)}, u32[]{:S(2)}, u32[]{:S(2)}) collective-permute-start(bf16[512,384]{1,0:T(8,128)(2,1)S(1)} %get-tuple-element.5), channel_id=1, source_target_pairs={{0,4},{4,8},{8,12},{12,16},{16,20},{20,24},{24,28},{1,5},{5,9},{9,... | collective-permute-start | bytes 1179656 | tf_op jit(solution)/shard_map/ppermute | solution.py:18
  152.0 1.5 collective-permute-start.3
  153.5 15.7 %collective-permute-done.2 = bf16[512,384]{1,0:T(8,128)(2,1)S(1)} collective-permute-done((bf16[512,384]{1,0:T(8,128)(2,1)S(1)}, bf16[512,384]{1,0:T(8,128)(2,1)S(1)}, u32[]{:S(2)}, u32[]{:S(2)}) %collective-permute-start.2) | collective-permute-done | bytes 393248 | tf_op jit(solution)/shard_map/ppermute | solution.py:18
  169.2 0.0 collective-permute-done.3
  169.2 1.6 pad_maximum_fusion
  170.9 0.0 all-gather.9.cloned.1.call-update
  170.9 35.5 %all-gather.11.cloned.1.call-done = bf16[3,1536,384]{2,1,0:T(8,128)(2,1)} async-done(((bf16[3,192,384]{2,1,0:T(8,128)(2,1)}), bf16[3,1536,384]{2,1,0:T(8,128)(2,1)}) %all-gather.11.cloned.1.call-update) | async-done | bytes 3538960 | tf_op jit(solution)/shard_map/all_gather | solution.py:41
  206.4 0.0 copy-start.3
  206.4 64.0 %all-gather.9.cloned.1.call-done = bf16[3072,1536]{1,0:T(8,128)(2,1)} async-done(((bf16[3072,384]{1,0:T(8,128)(2,1)}), bf16[3072,1536]{1,0:T(8,128)(2,1)}) %all-gather.9.cloned.1.call-update) | async-done | bytes 9437200 | tf_op jit(solution)/shard_map/all_gather | solution.py:34
  270.5 0.0 copy-start.1
  270.5 5.9 %fusion.2 = f32[2048,384]{1,0:T(8,128)S(1)} fusion(bf16[3072,1536]{1,0:T(8,128)(2,1)} %all-gather.9.cloned.1.call-done, bf16[3,1536,384]{2,1,0:T(8,128)(2,1)} %all-gather.11.cloned.1.call-done), kind=kOutput, calls=%fused_computation.2 | convolution fusion | flops 2415919104 | bytes 10616832 | tf_op jit(solution)/shard_map/dot_general | solution.py:44
  276.4 0.0 copy-done.3
  276.4 0.0 copy-done.1
  276.4 0.0 copy-start.7
  276.4 3.5 %fusion.4 = f32[2048,384]{1,0:T(8,128)S(1)} fusion(bf16[3072,1536]{1,0:T(8,128)(2,1)S(1)} %copy-done.1, bf16[3,1536,384]{2,1,0:T(8,128)(2,1)S(1)} %copy-done.3), kind=kOutput, calls=%fused_computation.4 | convolution fusion | flops 2415919104 | bytes 10616832 | tf_op jit(solution)/shard_map/dot_general | solution.py:44
  279.9 0.0 copy-done.7
  279.9 4.6 %fusion.29 = bf16[2048,384]{1,0:T(8,128)(2,1)} fusion(bf16[2048,384]{1,0:T(8,128)(2,1)S(1)} %copy-done.7, f32[2048,384]{1,0:T(8,128)S(1)} %fusion.4, f32[2048,384]{1,0:T(8,128)S(1)} %fusion.2, bf16[3072,1536]{1,0:T(8,128)(2,1)S(1)} %copy-done.1, bf16[3,1536,384]{2,1,0:T(8,128)(2,1)S(1)} %copy-done.3), kind=kOutput, calls=%fused_computation.35 | convolution fusion | flops 2419851264 | bytes 16908288 | tf_op jit(solution)/shard_map/dot_general | solution.py:44
  (1 shorter events, 0.0 us)
Async XLA Ops:
  6.5 71.5 %all-gather.7.cloned.1.call-start = ((), (), s32[]{:S(2)}) async-start(), calls=%async_computation.1 | async-start | bytes 3981312 | tf_op jit(solution)/shard_map/all_gather | solution.py:41
  7.3 126.1 %all-gather.5.cloned.1.call-start = ((), (), s32[]{:S(2)}) async-start(), calls=%async_computation | async-start | bytes 9830400 | tf_op jit(solution)/shard_map/all_gather | solution.py:34
  10.1 9.1 %collective-permute-start = (bf16[256,384]{1,0:T(8,128)(2,1)S(1)}, bf16[256,384]{1,0:T(8,128)(2,1)S(1)}, u32[]{:S(2)}, u32[]{:S(2)}) collective-permute-start(bf16[256,384]{1,0:T(8,128)(2,1)S(1)} %get-tuple-element.7), channel_id=1, source_target_pairs={{0,4},{4,8},{8,12},{12,16},{16,20},{20,24},{24,28},{1,5},{5,9},{9,... | collective-permute-start | bytes 589832 | tf_op jit(solution)/shard_map/ppermute | solution.py:18
  15.0 8.4 %collective-permute-start.1 = (bf16[256,384]{1,0:T(8,128)(2,1)S(1)}, bf16[256,384]{1,0:T(8,128)(2,1)S(1)}, u32[]{:S(2)}, u32[]{:S(2)}) collective-permute-start(bf16[256,384]{1,0:T(8,128)(2,1)S(1)} %get-tuple-element.8), channel_id=1, source_target_pairs={{4,0},{8,4},{12,8},{16,12},{20,16},{24,20},{28,24},{5,1},{9,5},{13... | collective-permute-start | bytes 589832 | tf_op jit(solution)/shard_map/ppermute | solution.py:20
  24.8 181.6 %all-gather.11.cloned.1.call-start = ((), (), s32[]{:S(2)}) async-start(), calls=%async_computation.3 | async-start | bytes 3981312 | tf_op jit(solution)/shard_map/all_gather | solution.py:41
  25.6 244.9 %all-gather.9.cloned.1.call-start = ((), (), s32[]{:S(2)}) async-start(), calls=%async_computation.2 | async-start | bytes 11796480 | tf_op jit(solution)/shard_map/all_gather | solution.py:34
  78.0 61.2 %copy-start.4 = (bf16[3,1536,384]{2,1,0:T(8,128)(2,1)S(1)}, bf16[3,1536,384]{2,1,0:T(8,128)(2,1)}, u32[]{:S(2)}) copy-start(bf16[3,1536,384]{2,1,0:T(8,128)(2,1)} %all-gather.7.cloned.1.call-done) | copy-start | bytes 10616836
  133.3 6.0 %copy-start.2 = (bf16[2560,1536]{1,0:T(8,128)(2,1)S(1)}, bf16[2560,1536]{1,0:T(8,128)(2,1)}, u32[]{:S(2)}) copy-start(bf16[2560,1536]{1,0:T(8,128)(2,1)} %all-gather.5.cloned.1.call-done) | copy-start | bytes 23592964
  139.3 3.5 %copy-start = (bf16[2048,384]{1,0:T(8,128)(2,1)S(1)}, bf16[2048,384]{1,0:T(8,128)(2,1)}, u32[]{:S(2)}) copy-start(bf16[2048,384]{1,0:T(8,128)(2,1)} %param.7) | copy-start | bytes 4718596
  139.3 3.5 %copy-start.5 = (f32[384]{0:T(512)S(1)}, f32[384]{0:T(512)}, u32[]{:S(2)}) copy-start(f32[384]{0:T(512)} %param.12) | copy-start | bytes 4612
  139.3 3.5 %copy-start.6 = (f32[384]{0:T(512)S(1)}, f32[384]{0:T(512)}, u32[]{:S(2)}) copy-start(f32[384]{0:T(512)} %param.11) | copy-start | bytes 4612
  148.6 20.6 %collective-permute-start.2 = (bf16[512,384]{1,0:T(8,128)(2,1)S(1)}, bf16[512,384]{1,0:T(8,128)(2,1)S(1)}, u32[]{:S(2)}, u32[]{:S(2)}) collective-permute-start(bf16[512,384]{1,0:T(8,128)(2,1)S(1)} %get-tuple-element.5), channel_id=1, source_target_pairs={{0,4},{4,8},{8,12},{12,16},{16,20},{20,24},{24,28},{1,5},{5,9},{9,... | collective-permute-start | bytes 1179656 | tf_op jit(solution)/shard_map/ppermute | solution.py:18
  152.0 17.2 %collective-permute-start.3 = (bf16[512,384]{1,0:T(8,128)(2,1)S(1)}, bf16[512,384]{1,0:T(8,128)(2,1)S(1)}, u32[]{:S(2)}, u32[]{:S(2)}) collective-permute-start(bf16[512,384]{1,0:T(8,128)(2,1)S(1)} %get-tuple-element.6), channel_id=1, source_target_pairs={{4,0},{8,4},{12,8},{16,12},{20,16},{24,20},{28,24},{5,1},{9,5},{13... | collective-permute-start | bytes 1179656 | tf_op jit(solution)/shard_map/ppermute | solution.py:20
  206.4 70.0 %copy-start.3 = (bf16[3,1536,384]{2,1,0:T(8,128)(2,1)S(1)}, bf16[3,1536,384]{2,1,0:T(8,128)(2,1)}, u32[]{:S(2)}) copy-start(bf16[3,1536,384]{2,1,0:T(8,128)(2,1)} %all-gather.11.cloned.1.call-done) | copy-start | bytes 10616836
  270.5 6.0 %copy-start.1 = (bf16[3072,1536]{1,0:T(8,128)(2,1)S(1)}, bf16[3072,1536]{1,0:T(8,128)(2,1)}, u32[]{:S(2)}) copy-start(bf16[3072,1536]{1,0:T(8,128)(2,1)} %all-gather.9.cloned.1.call-done) | copy-start | bytes 28311556
  276.4 3.5 %copy-start.7 = (bf16[2048,384]{1,0:T(8,128)(2,1)S(1)}, bf16[2048,384]{1,0:T(8,128)(2,1)}, u32[]{:S(2)}) copy-start(bf16[2048,384]{1,0:T(8,128)(2,1)} %get-tuple-element.10) | copy-start | bytes 4718596
Sparse Core Ops, SparseCore 0:
  9.5 68.4 all-gather.6
  79.6 53.6 all-gather.4
  135.5 70.8 all-gather.10
  207.8 62.5 all-gather.8
where the time goes:
time: 291 us
  waiting for transfers between devices  231 us (79%)
  matrix products  29.1 us (10%)
  between operations  13.3 us (5%)
  starting transfers between devices  11.2 us (4%)
  other arithmetic  5.82 us (2%)
    all_gather x2, waiting for transfers between devices, widen(): return lax.all_gather(narrow, 'wt', axis=1, tiled=True)  119 us
    all_gather x2, waiting for transfers between devices, conv_layer(): kernel = lax.all_gather(weight, 'seq', axis=1, tiled=True)  87.9 us
    dot_general x6, matrix products, conv_layer(): jnp.dot(extended[tap * reach:tap * reach + count], kernel[tap], preferred...  29.1 us
    ppermute x2, waiting for transfers between devices, padded(): lax.ppermute(tail, axis, [(i, (i + 1) % count) for i in range(ends)])  18.6 us
    ppermute x2, starting transfers between devices, padded(): lax.ppermute(tail, axis, [(i, (i + 1) % count) for i in range(ends)])  8.28 us
  transfers between devices with their start and end apart: 8, of which 7 were waited for; matrix products, arithmetic and copies ran while one was open for 7% of the time, Pallas kernels for 0%

commit v1 on v0

v1 whole, which is shorter than its diff:
```python
import functools

import jax
import jax.numpy as jnp
from jax import lax
from jax.experimental import pallas as pl
from jax.experimental.pallas import tpu as pltpu
from jax.sharding import PartitionSpec as P

DILATION_FIRST = 256
DILATION_SECOND = 512
CHUNK = 256
TAPS = 3


def tower_kernel(
    n, m, x_ref, s1_ref, b1_ref, w1_ref, s2_ref, b2_ref, w2_ref, out_ref,
    hid1, hid2, wb, one,
    s_p, r_p, s_q, r_q, s_y, r_y, s_x, r_x, s_c, r_c, s_f, r_f, s_h, r_h,
):
    s = lax.axis_index("seq")
    w = lax.axis_index("wt")
    lines = n // 2
    z, y = s // 2, lax.rem(s, 2)
    x_peer = lax.rem(w + m // 2, m)
    c_peer = w + 1 - 2 * lax.rem(w, 2)
    xc_peer = lax.rem(c_peer + m // 2, m)
    y_peer = s + 1 - 2 * y
    rows, cols = x_ref.shape
    kr = w1_ref.shape[1]
    nc = rows // CHUNK
    reach = (DILATION_FIRST // CHUNK, DILATION_SECOND // CHUNK)
    hids = (hid1, hid2)
    scales = (s1_ref, s2_ref)
    shifts = (b1_ref, b2_ref)
    has_prev, has_next = s > 0, s < n - 1
    up, down = z < lines - 1, z > 0
    steps = ((1, up), (-1, down))

    def rdma(src, dst, ss, rs, ds, dw):
        return pltpu.make_async_remote_copy(
            src_ref=src, dst_ref=dst, send_sem=ss, recv_sem=rs,
            device_id=(ds, dw), device_id_type=pl.DeviceIdType.MESH,
        )

    def span(e):
        return pl.ds(pl.multiple_of(e * CHUNK, CHUNK), CHUNK)

    def lane(j):
        return pl.ds(pl.multiple_of(j * cols, cols), cols)

    def krows(zz, yy):
        return pl.ds(pl.multiple_of((zz * 2 + yy) * kr, kr), kr)

    def msg_p(l, zz, d):
        ref = wb.at[l, :, krows(zz, y), :]
        i = 0 if d > 0 else 1
        return rdma(ref, ref, s_p.at[i, l, zz], r_p.at[l, zz], s + 2 * d, w)

    def msg_q(l, zz, d):
        ref = wb.at[l, pl.ds(TAPS - 1, 1), krows(zz, 1 - y), :]
        i = 0 if d > 0 else 1
        return rdma(ref, ref, s_q.at[i, l, zz], r_q.at[l, zz], s + 2 * d, w)

    def msg_y(l, zz, yy, count):
        ref = wb.at[l, pl.ds(0, count), krows(zz, yy), :]
        return rdma(ref, ref, s_y.at[l, zz], r_y.at[l, zz], y_peer, w)

    def weights_start(l):
        for d, there in steps:
            @pl.when(there)
            def _():
                msg_p(l, z, d).start()
        msg_y(l, z, y, TAPS).start()

    def weights_pair(l):
        msg_y(l, z, 1 - y, TAPS).wait_recv()
        for d, there in steps:
            @pl.when(there)
            def _():
                msg_q(l, z, d).start()

    def weights_step(l, k):
        for d, there in steps:
            zz = z - d * k
            onward = there

            @pl.when(jnp.logical_and(zz >= 0, zz < lines))
            def _():
                msg_p(l, zz, d).wait_recv()

                @pl.when(onward)
                def _():
                    msg_p(l, zz, d).start()

                msg_y(l, zz, y, TAPS - 1).start()
                msg_q(l, zz, d).wait_recv()

                @pl.when(onward)
                def _():
                    msg_q(l, zz, d).start()

    def weights_finish(l):
        for k in range(1, lines):
            for d in (1, -1):
                zz = z - d * k

                @pl.when(jnp.logical_and(zz >= 0, zz < lines))
                def _():
                    msg_y(l, zz, 1 - y, TAPS - 1).wait_recv()

    def weights_drain(l):
        msg_y(l, z, y, TAPS).wait_send()
        for k in range(lines):
            for d, there in steps:
                zz = z - d * k

                @pl.when(jnp.logical_and(zz >= 0, zz < lines))
                def _():
                    if k:
                        msg_y(l, zz, y, TAPS - 1).wait_send()

                    @pl.when(there)
                    def _():
                        msg_p(l, zz, d).wait_send()
                        msg_q(l, zz, d).wait_send()

    def msg_x(l, e, j):
        ref = hids[l].at[span(e), lane(j)]
        return rdma(ref, ref, s_x.at[l, e], r_x.at[l, e], s, x_peer)

    def msg_c(l, e, j):
        ref = hids[l].at[span(e), lane(j)]
        return rdma(ref, ref, s_c.at[l, e], r_c.at[l, e], s, c_peer)

    def msg_f(l, e, j):
        ref = hids[l].at[span(e), lane(j)]
        return rdma(ref, ref, s_f.at[l, e], r_f.at[l, e], s, c_peer)

    def msg_h(l, src, dst, d):
        hid = hids[l]
        return rdma(
            hid.at[span(src), lane(w)], hid.at[span(dst), lane(w)],
            s_h.at[l, dst], r_h.at[l, dst], s + d, w,
        )

    def emit(l, c, state):
        reach_l = reach[l]
        value = state.astype(jnp.float32) * scales[l][...] + shifts[l][...]
        hidden = jax.nn.gelu(value, approximate=True).astype(jnp.bfloat16)
        e = c + reach_l
        hids[l][span(e), lane(w)] = hidden

        @pl.when(jnp.logical_and(c < reach_l, has_prev))
        def _():
            msg_h(l, e, nc + e, -1).start()

        @pl.when(jnp.logical_and(c >= nc - reach_l, has_next))
        def _():
            msg_h(l, e, e - nc, 1).start()

        msg_x(l, e, w).start()
        msg_c(l, e, w).start()

    def halos(l):
        d = reach[l]
        return [(e, has_prev) for e in range(d)] + [
            (nc + d + e, has_next) for e in range(d)
        ]

    def halo_arrive(l, e, there):
        @pl.when(there)
        def _():
            msg_h(l, e, e, 1).wait_recv()
            msg_x(l, e, w).start()
            msg_c(l, e, w).start()

        @pl.when(jnp.logical_not(there))
        def _():
            hids[l][span(e), :] = jnp.zeros((CHUNK, m * cols), jnp.bfloat16)

    def forward(l, e, there=None):
        def go():
            msg_x(l, e, x_peer).wait_recv()
            msg_f(l, e, x_peer).start()

        if there is None:
            go()
        else:
            pl.when(there)(go)

    def ready(l, e, there=None):
        def go():
            msg_c(l, e, c_peer).wait_recv()
            msg_f(l, e, xc_peer).wait_recv()

        if there is None:
            go()
        else:
            pl.when(there)(go)

    def sent(l):
        d = reach[l]

        def one_chunk(e):
            msg_x(l, e, w).wait_send()
            msg_c(l, e, w).wait_send()
            msg_f(l, e, x_peer).wait_send()

        for e, there in halos(l):
            @pl.when(there)
            def _():
                one_chunk(e)
        for e in range(d, nc + d):
            one_chunk(e)
        for e in range(d):
            @pl.when(has_prev)
            def _():
                msg_h(l, d + e, nc + d + e, -1).wait_send()

            @pl.when(has_next)
            def _():
                msg_h(l, nc + e, e, 1).wait_send()

    def own_order(l):
        d = reach[l]
        return [(i + nc - d) % nc + d for i in range(nc)]

    def conv(l, c, state):
        d = reach[l]
        total = jnp.zeros((CHUNK, cols), jnp.float32)
        for tap in range(TAPS):
            total = total + jnp.dot(
                hids[l][span(c + tap * d), :], wb[l, tap],
                preferred_element_type=jnp.float32,
            )
        return (state.astype(jnp.float32) + total).astype(jnp.bfloat16)

    barrier = pltpu.get_barrier_semaphore()
    peers = [
        (True, y_peer, w), (True, s, x_peer), (True, s, c_peer),
        (up, s + 2, w), (down, s - 2, w), (has_next, s + 1, w), (has_prev, s - 1, w),
    ]
    expected = 3
    for there, ds, dw in peers:
        def greet(ds=ds, dw=dw):
            pl.semaphore_signal(
                barrier, inc=1, device_id=(ds, dw), device_id_type=pl.DeviceIdType.MESH
            )

        if there is True:
            greet()
        else:
            pl.when(there)(greet)
            expected = expected + there.astype(jnp.int32)
    wb[0, :, krows(z, y), :] = w1_ref[...]
    wb[1, :, krows(z, y), :] = w2_ref[...]
    pl.semaphore_wait(barrier, expected)

    weights_start(0)

    @pl.loop(0, nc)
    def _(i):
        c = lax.rem(i + nc - reach[0], nc)
        emit(0, c, x_ref[span(c), :])

    for e, there in halos(0):
        halo_arrive(0, e, there)
    weights_pair(0)
    k = 1
    incoming = [(e, None) for e in own_order(0)] + halos(0)
    for i, (e, there) in enumerate(incoming):
        forward(0, e, there)
        if i % 3 == 1 and k < lines:
            weights_step(0, k)
            k += 1
    for k in range(k, lines):
        weights_step(0, k)
    weights_start(1)
    weights_finish(0)
    for e, there in incoming:
        ready(0, e, there)

    @pl.loop(0, nc)
    def _(i):
        c = lax.rem(i + nc - reach[1], nc)
        state = conv(0, c, x_ref[span(c), :])
        one[span(c), :] = state
        emit(1, c, state)

    weights_pair(1)
    own, edge = own_order(1), halos(1)
    k = 1
    for i, e in enumerate(own):
        forward(1, e)
        if i >= 2 and i - 2 < len(edge):
            halo_arrive(1, *edge[i - 2])
        if i % 3 == 1 and k < lines:
            weights_step(1, k)
            k += 1
    for i in range(max(len(own) - 2, 0), len(edge)):
        halo_arrive(1, *edge[i])
    for k in range(k, lines):
        weights_step(1, k)
    for e, there in edge:
        forward(1, e, there)
    weights_finish(1)
    for e in own:
        ready(1, e)
    for e, there in edge:
        ready(1, e, there)

    @pl.loop(0, nc)
    def _(i):
        c = lax.rem(i + reach[1], nc)
        out_ref[span(c), :] = conv(1, c, one[span(c), :])

    for l in range(2):
        sent(l)
        weights_drain(l)


def shards(n, m, x, s1, b1, w1, s2, b2, w2):
    rows, cols = x.shape
    channels = m * cols
    lines = n // 2
    ext = rows // CHUNK + 2 * (DILATION_SECOND // CHUNK)
    dma = pltpu.SemaphoreType.DMA
    vmem = pl.BlockSpec(memory_space=pltpu.VMEM)
    return pl.pallas_call(
        functools.partial(tower_kernel, n, m),
        out_shape=jax.ShapeDtypeStruct((rows, cols), jnp.bfloat16),
        in_specs=[vmem] * 7,
        out_specs=vmem,
        scratch_shapes=[
            pltpu.VMEM((rows + 2 * DILATION_FIRST, channels), jnp.bfloat16),
            pltpu.VMEM((rows + 2 * DILATION_SECOND, channels), jnp.bfloat16),
            pltpu.VMEM((2, TAPS, channels, cols), jnp.bfloat16),
            pltpu.VMEM((rows, cols), jnp.bfloat16),
            dma((2, 2, lines)), dma((2, lines)),
            dma((2, 2, lines)), dma((2, lines)),
            dma((2, lines)), dma((2, lines)),
        ] + [dma((2, ext))] * 8,
        compiler_params=pltpu.CompilerParams(
            collective_id=0, has_side_effects=True, vmem_limit_bytes=56 * 1024 * 1024
        ),
        cost_estimate=pl.CostEstimate(
            flops=4 * TAPS * rows * channels * cols,
            bytes_accessed=4 * rows * cols + 4 * TAPS * w1.shape[1] * cols,
            transcendentals=2 * rows * cols,
        ),
    )(x, s1[None, :], b1[None, :], w1, s2[None, :], b2[None, :], w2)


def solution(mesh):
    placed = (
        P("seq", "wt"),
        P("wt"),
        P("wt"),
        P(None, "seq", "wt"),
        P("wt"),
        P("wt"),
        P(None, "seq", "wt"),
    )
    n, m = mesh.shape["seq"], mesh.shape["wt"]
    return jax.shard_map(
        functools.partial(shards, n, m), mesh=mesh, in_specs=placed,
        out_specs=P("seq", "wt"), check_vma=False,
    )
```

time: 291 us -> 136 us (0.47)
  the two profiles are of different devices: /device:TPU:0 before, /device:TPU:5 now
where the time goes in v1:
time: 136 us; the launch traced here: 135 us
  Pallas kernels  128 us (94%)
  local copies, waits for them, and re-layouts  7.71 us (6%)
    pallas_call x1, Pallas kernels, shards(): pl.pallas_call(functools.partial(tower_kernel, n, m), out_shape=jax.Shape...  128 us

profile of v1, /device:TPU:5, one launch (start us, length us, event | category | flops | bytes accessed | tf_op | source)
XLA Modules:
  0.0 135.5 jit_solution(4498949791313686146)
XLA Ops:
  0.0 1.2 broadcast_in_dim.12.s1_ref
  1.2 1.3 broadcast_in_dim.13.b1_ref
  2.5 1.3 broadcast_in_dim.14.s2_ref
  3.8 1.2 broadcast_in_dim.15.b2_ref
  5.0 127.8 %shard_map.73 = bf16[2048,384]{1,0:T(8,128)(2,1)} custom-call(bf16[2048,384]{1,0:T(8,128)(2,1)} %x_ref.1, f32[1,384]{1,0:T(1,128)} %broadcast_in_dim.12.s1_ref, f32[1,384]{1,0:T(1,128)} %broadcast_in_dim.13.b1_ref, bf16[3,192,384]{2,1,0:T(8,128)(2,1)} %w1_ref.1, f32[1,384]{1,0:T(1,128)} %broadcast_in_dim.14.s2_ref, f32[1,384]{1,0:T(1,128)} %broadcast_in_dim.15.b2_ref, ...), custom_call_target="tpu_custom_call" | custom-call | flops 14495514624 | bytes 4030464 | tf_op jit(solution)/shard_map/pallas_call | solution.py:330
  132.8 2.7 %copy.9 = bf16[2048,384]{1,0:T(8,128)(2,1)} copy(bf16[2048,384]{1,0:T(8,128)(2,1)} %shard_map.73) | data formatting | bytes 3145728

commit v2 on v1

--- a/solution.py
+++ b/solution.py
@@ -15,7 +15,7 @@
 
 def tower_kernel(
     n, m, x_ref, s1_ref, b1_ref, w1_ref, s2_ref, b2_ref, w2_ref, out_ref,
-    hid1, hid2, wb, one,
+    hid1, hid2, wb, one, part_out, part_in, s_g, r_g,
     s_p, r_p, s_q, r_q, s_y, r_y, s_x, r_x, s_c, r_c, s_f, r_f, s_h, r_h,
 ):
     s = lax.axis_index("seq")
@@ -30,6 +30,7 @@
     kr = w1_ref.shape[1]
     nc = rows // CHUNK
     reach = (DILATION_FIRST // CHUNK, DILATION_SECOND // CHUNK)
+    edge = (0, reach[1])
     hids = (hid1, hid2)
     scales = (s1_ref, s2_ref)
     shifts = (b1_ref, b2_ref)
@@ -145,28 +146,30 @@
         )
 
     def emit(l, c, state):
-        reach_l = reach[l]
-        value = state.astype(jnp.float32) * scales[l][...] + shifts[l][...]
+        value = state.astype(jnp.float32) * scales[l][...][None, :] + shifts[l][...][None, :]
         hidden = jax.nn.gelu(value, approximate=True).astype(jnp.bfloat16)
-        e = c + reach_l
+        e = c + edge[l]
         hids[l][span(e), lane(w)] = hidden
-
-        @pl.when(jnp.logical_and(c < reach_l, has_prev))
-        def _():
-            msg_h(l, e, nc + e, -1).start()
-
-        @pl.when(jnp.logical_and(c >= nc - reach_l, has_next))
-        def _():
-            msg_h(l, e, e - nc, 1).start()
+        if edge[l]:
+            @pl.when(jnp.logical_and(c < edge[l], has_prev))
+            def _():
+                msg_h(l, e, nc + e, -1).start()
+
+            @pl.when(jnp.logical_and(c >= nc - edge[l], has_next))
+            def _():
+                msg_h(l, e, e - nc, 1).start()
 
         msg_x(l, e, w).start()
         msg_c(l, e, w).start()
 
     def halos(l):
-        d = reach[l]
-        return [(e, has_prev) for e in range(d)] + [
-            (nc + d + e, has_next) for e in range(d)
-        ]
+        out = []
+        for c in makes:
+            if c >= nc - edge[l]:
+                out.append((c - (nc - edge[l]), has_prev))
+            if c < edge[l]:
+                out.append((nc + edge[l] + c, has_next))
+        return out
 
     def halo_arrive(l, e, there):
         @pl.when(there)
@@ -200,7 +203,7 @@
             pl.when(there)(go)
 
     def sent(l):
-        d = reach[l]
+        d = edge[l]
 
         def one_chunk(e):
             msg_x(l, e, w).wait_send()
@@ -222,19 +225,20 @@
             def _():
                 msg_h(l, nc + e, e, 1).wait_send()
 
-    def own_order(l):
-        d = reach[l]
-        return [(i + nc - d) % nc + d for i in range(nc)]
-
-    def conv(l, c, state):
-        d = reach[l]
-        total = jnp.zeros((CHUNK, cols), jnp.float32)
-        for tap in range(TAPS):
-            total = total + jnp.dot(
-                hids[l][span(c + tap * d), :], wb[l, tap],
-                preferred_element_type=jnp.float32,
-            )
+    def product(l, e, tap):
+        return jnp.dot(
+            hids[l][span(e), :], wb[l, tap], preferred_element_type=jnp.float32
+        )
+
+    def joined(state, total):
         return (state.astype(jnp.float32) + total).astype(jnp.bfloat16)
+
+    def msg_g(i):
+        return rdma(
+            part_out.at[i], part_in.at[i], s_g.at[i], r_g.at[i], s + (1 if i == 0 else -1), w
+        )
+
+    makes = [1 + (i + nc - 3) % (nc - 2) for i in range(nc - 2)] + [0, nc - 1]
 
     barrier = pltpu.get_barrier_semaphore()
     peers = [
@@ -261,60 +265,87 @@
 
     @pl.loop(0, nc)
     def _(i):
-        c = lax.rem(i + nc - reach[0], nc)
-        emit(0, c, x_ref[span(c), :])
-
-    for e, there in halos(0):
-        halo_arrive(0, e, there)
+        emit(0, i, x_ref[span(i), :])
+
     weights_pair(0)
     k = 1
-    incoming = [(e, None) for e in own_order(0)] + halos(0)
-    for i, (e, there) in enumerate(incoming):
-        forward(0, e, there)
-        if i % 3 == 1 and k < lines:
+    for e in range(nc):
+        forward(0, e)
+        if e % 3 == 1 and k < lines:
             weights_step(0, k)
             k += 1
     for k in range(k, lines):
         weights_step(0, k)
     weights_start(1)
     weights_finish(0)
-    for e, there in incoming:
-        ready(0, e, there)
-
-    @pl.loop(0, nc)
-    def _(i):
-        c = lax.rem(i + nc - reach[1], nc)
-        state = conv(0, c, x_ref[span(c), :])
+    for e in range(nc):
+        ready(0, e)
+
+    part_out[0] = product(0, nc - 1, 0).astype(jnp.bfloat16)
+    part_out[1] = product(0, 0, TAPS - 1).astype(jnp.bfloat16)
+    for i, out, back in ((0, has_next, has_prev), (1, has_prev, has_next)):
+        pl.when(out)(msg_g(i).start)
+
+        @pl.when(jnp.logical_not(back))
+        def _():
+            part_in[i] = jnp.zeros((CHUNK, cols), jnp.bfloat16)
+
+    def make(c, total):
+        state = joined(x_ref[span(c), :], total)
         one[span(c), :] = state
         emit(1, c, state)
 
-    weights_pair(1)
-    own, edge = own_order(1), halos(1)
+    @pl.loop(0, nc - 2)
+    def _(i):
+        c = 1 + lax.rem(i + nc - 3, nc - 2)
+        make(c, product(0, c - 1, 0) + product(0, c, 1) + product(0, c + 1, 2))
+
+    for i, c, other, tap, back in ((0, 0, 1, 2, has_prev), (1, nc - 1, nc - 2, 0, has_next)):
+        total = product(0, c, 1) + product(0, other, tap)
+        pl.when(back)(msg_g(i).wait_recv)
+        make(c, total + part_in[i].astype(jnp.float32))
+
+    own = [(c + edge[1], None) for c in makes]
+    ends = halos(1)
+    arrived = set()
+    left = list(range(nc))
+
+    def conv_ready():
+        for c in list(left):
+            needs = [c + tap * reach[1] for tap in range(TAPS)]
+            if arrived.issuperset(needs):
+                left.remove(c)
+                total = product(1, needs[0], 0) + product(1, needs[1], 1) + product(1, needs[2], 2)
+                out_ref[span(c), :] = joined(one[span(c), :], total)
+
     k = 1
-    for i, e in enumerate(own):
+    pending = list(ends)
+    for i, (e, _) in enumerate(own):
         forward(1, e)
-        if i >= 2 and i - 2 < len(edge):
-            halo_arrive(1, *edge[i - 2])
-        if i % 3 == 1 and k < lines:
+        if i == 1:
+            weights_pair(1)
+        if i % 3 == 2 and k < lines:
             weights_step(1, k)
             k += 1
-    for i in range(max(len(own) - 2, 0), len(edge)):
-        halo_arrive(1, *edge[i])
+        if i >= 5 and pending:
+            halo_arrive(1, *pending.pop(0))
+    for e, there in pending:
+        halo_arrive(1, e, there)
     for k in range(k, lines):
         weights_step(1, k)
-    for e, there in edge:
+    weights_finish(1)
+    for e, _ in own:
+        ready(1, e)
+        arrived.add(e)
+    conv_ready()
+    for e, there in ends:
         forward(1, e, there)
-    weights_finish(1)
-    for e in own:
-        ready(1, e)
-    for e, there in edge:
         ready(1, e, there)
-
-    @pl.loop(0, nc)
-    def _(i):
-        c = lax.rem(i + reach[1], nc)
-        out_ref[span(c), :] = conv(1, c, one[span(c), :])
-
+        arrived.add(e)
+        conv_ready()
+
+    for i, out in ((0, has_next), (1, has_prev)):
+        pl.when(out)(msg_g(i).wait_send)
     for l in range(2):
         sent(l)
         weights_drain(l)
@@ -333,10 +364,13 @@
         in_specs=[vmem] * 7,
         out_specs=vmem,
         scratch_shapes=[
-            pltpu.VMEM((rows + 2 * DILATION_FIRST, channels), jnp.bfloat16),
+            pltpu.VMEM((rows, channels), jnp.bfloat16),
             pltpu.VMEM((rows + 2 * DILATION_SECOND, channels), jnp.bfloat16),
             pltpu.VMEM((2, TAPS, channels, cols), jnp.bfloat16),
             pltpu.VMEM((rows, cols), jnp.bfloat16),
+            pltpu.VMEM((2, CHUNK, cols), jnp.bfloat16),
+            pltpu.VMEM((2, CHUNK, cols), jnp.bfloat16),
+            dma((2,)), dma((2,)),
             dma((2, 2, lines)), dma((2, lines)),
             dma((2, 2, lines)), dma((2, lines)),
             dma((2, lines)), dma((2, lines)),
@@ -349,7 +383,7 @@
             bytes_accessed=4 * rows * cols + 4 * TAPS * w1.shape[1] * cols,
             transcendentals=2 * rows * cols,
         ),
-    )(x, s1[None, :], b1[None, :], w1, s2[None, :], b2[None, :], w2)
+    )(x, s1, b1, w1, s2, b2, w2)
 
 
 def solution(mesh):

time: 136 us -> 129 us (0.949)
  the two profiles are of different devices: /device:TPU:5 before, /device:TPU:0 now
where the time goes in v2:
time: 129 us
  Pallas kernels  126 us (98%)
  local copies, waits for them, and re-layouts  2.71 us (2%)
    pallas_call x1, Pallas kernels, shards(): pl.pallas_call(functools.partial(tower_kernel, n, m), out_shape=jax.Shape...  126 us
    unnamed x1, local copies, waits for them, and re-layouts  2.71 us

profile of v2, /device:TPU:0, one launch (start us, length us, event | category | flops | bytes accessed | tf_op | source)
XLA Modules:
  0.0 128.7 jit_solution(426537546359755158)
XLA Ops:
  0.0 126.0 %shard_map.73 = bf16[2048,384]{1,0:T(8,128)(2,1)} custom-call(bf16[2048,384]{1,0:T(8,128)(2,1)} %x_ref.1, f32[384]{0:T(512)} %s1_ref.1, f32[384]{0:T(512)} %b1_ref.1, bf16[3,192,384]{2,1,0:T(8,128)(2,1)} %w1_ref.1, f32[384]{0:T(512)} %s2_ref.1, f32[384]{0:T(512)} %b2_ref.1, bf16[3,192,384]{2,1,0:T(8,128)(2,1)} %w2_ref.1), custom_call_target="tpu_custom_call" | custom-call | flops 14495514624 | bytes 4030464 | tf_op jit(solution)/shard_map/pallas_call | solution.py:361
  126.0 2.7 %copy.9 = bf16[2048,384]{1,0:T(8,128)(2,1)} copy(bf16[2048,384]{1,0:T(8,128)(2,1)} %shard_map.73) | data formatting | bytes 3145728

commit v3 on v0

v3 whole, which is shorter than its diff:
```python
import functools

import jax
import jax.numpy as jnp
from jax import lax
from jax.experimental import pallas as pl
from jax.experimental.pallas import tpu as pltpu
from jax.sharding import PartitionSpec as P

DILATION_FIRST = 256
DILATION_SECOND = 512
CHUNK = 256
TAPS = 3
ORDER = (0, 2, 1)
LAST = ORDER[-1]


def tower_kernel(
    n, m, x_ref, s1_ref, b1_ref, w1_ref, s2_ref, b2_ref, w2_ref, out_ref,
    hid1, hid2, wb, one, acc, part_out, part_in, s_g, r_g,
    s_p, r_p, s_q, r_q, s_y, r_y, s_x, r_x, s_c, r_c, s_f, r_f,
):
    s = lax.axis_index("seq")
    w = lax.axis_index("wt")
    lines = n // 2
    z, y = s // 2, lax.rem(s, 2)
    x_peer = lax.rem(w + m // 2, m)
    c_peer = w + 1 - 2 * lax.rem(w, 2)
    xc_peer = lax.rem(c_peer + m // 2, m)
    y_peer = s + 1 - 2 * y
    rows, cols = x_ref.shape
    kr = w1_ref.shape[1]
    nc = rows // CHUNK
    reach = (DILATION_FIRST // CHUNK, DILATION_SECOND // CHUNK)
    hids = (hid1, hid2)
    scales = (s1_ref, s2_ref)
    shifts = (b1_ref, b2_ref)
    has_prev, has_next = s > 0, s < n - 1
    up, down = z < lines - 1, z > 0
    steps = ((1, up), (-1, down))

    def rdma(src, dst, ss, rs, ds, dw):
        return pltpu.make_async_remote_copy(
            src_ref=src, dst_ref=dst, send_sem=ss, recv_sem=rs,
            device_id=(ds, dw), device_id_type=pl.DeviceIdType.MESH,
        )

    def span(e):
        return pl.ds(pl.multiple_of(e * CHUNK, CHUNK), CHUNK)

    def lane(j):
        return pl.ds(pl.multiple_of(j * cols, cols), cols)

    def krows(zz, yy):
        return pl.ds(pl.multiple_of((zz * 2 + yy) * kr, kr), kr)

    def msg_p(l, tap, zz, d):
        ref = wb.at[l, tap, krows(zz, y), :]
        i, j = (0 if d > 0 else 1), l * TAPS + tap
        return rdma(ref, ref, s_p.at[i, j, zz], r_p.at[j, zz], s + 2 * d, w)

    def msg_q(l, zz, d):
        ref = wb.at[l, LAST, krows(zz, 1 - y), :]
        i = 0 if d > 0 else 1
        return rdma(ref, ref, s_q.at[i, l, zz], r_q.at[l, zz], s + 2 * d, w)

    def msg_y(l, tap, zz, yy):
        ref = wb.at[l, tap, krows(zz, yy), :]
        j = l * TAPS + tap
        return rdma(ref, ref, s_y.at[j, zz], r_y.at[j, zz], y_peer, w)

    def weights_start(l, tap):
        if tap == ORDER[1]:
            msg_y(l, LAST, z, y).start()
        if tap == LAST:
            msg_y(l, LAST, z, 1 - y).wait_recv()
        else:
            msg_y(l, tap, z, y).start()
        for d, there in steps:
            @pl.when(there)
            def _():
                msg_p(l, tap, z, d).start()
                if tap == LAST:
                    msg_q(l, z, d).start()

    def weights_step(l, tap, k):
        for d, there in steps:
            zz = z - d * k

            @pl.when(jnp.logical_and(zz >= 0, zz < lines))
            def _():
                msg_p(l, tap, zz, d).wait_recv()
                pl.when(there)(msg_p(l, tap, zz, d).start)
                if tap == LAST:
                    msg_q(l, zz, d).wait_recv()
                    pl.when(there)(msg_q(l, zz, d).start)
                else:
                    msg_y(l, tap, zz, y).start()

    def weights_finish(l, tap):
        if tap == LAST:
            return
        msg_y(l, tap, z, 1 - y).wait_recv()
        for k in range(1, lines):
            for d in (1, -1):
                zz = z - d * k
                pl.when(jnp.logical_and(zz >= 0, zz < lines))(
                    msg_y(l, tap, zz, 1 - y).wait_recv
                )

    def weights_drain(l):
        for tap in range(TAPS):
            msg_y(l, tap, z, y).wait_send()
            for k in range(lines):
                for d, there in steps:
                    zz = z - d * k

                    @pl.when(jnp.logical_and(zz >= 0, zz < lines))
                    def _():
                        if k and tap != LAST:
                            msg_y(l, tap, zz, y).wait_send()

                        @pl.when(there)
                        def _():
                            msg_p(l, tap, zz, d).wait_send()
                            if tap == LAST:
                                msg_q(l, zz, d).wait_send()

    def msg_x(l, e, j):
        ref = hids[l].at[span(e), lane(j)]
        return rdma(ref, ref, s_x.at[l, e], r_x.at[l, e], s, x_peer)

    def msg_c(l, e, j):
        ref = hids[l].at[span(e), lane(j)]
        return rdma(ref, ref, s_c.at[l, e], r_c.at[l, e], s, c_peer)

    def msg_f(l, e, j):
        ref = hids[l].at[span(e), lane(j)]
        return rdma(ref, ref, s_f.at[l, e], r_f.at[l, e], s, c_peer)

    def emit(l, c, state):
        value = state.astype(jnp.float32) * scales[l][...][None, :] + shifts[l][...][None, :]
        hids[l][span(c), lane(w)] = jax.nn.gelu(value, approximate=True).astype(jnp.bfloat16)
        msg_x(l, c, w).start()
        msg_c(l, c, w).start()

    def forward(l, e):
        msg_x(l, e, x_peer).wait_recv()
        msg_f(l, e, x_peer).start()

    def ready(l, e):
        msg_c(l, e, c_peer).wait_recv()
        msg_f(l, e, xc_peer).wait_recv()

    def sent(l):
        for e in range(nc):
            msg_x(l, e, w).wait_send()
            msg_c(l, e, w).wait_send()
            msg_f(l, e, x_peer).wait_send()

    def product(l, e, tap):
        return jnp.dot(
            hids[l][span(e), :], wb[l, tap], preferred_element_type=jnp.float32
        )

    states = (x_ref, one)

    def msg_g(l, i):
        ref = pl.ds(0, reach[l] * CHUNK)
        return rdma(
            part_out.at[l, i, ref, :], part_in.at[l, i, ref, :],
            s_g.at[l, i], r_g.at[l, i], s + (1 if i == 0 else -1), w,
        )

    def tap_first(l, lo, hi):
        d = reach[l]
        cut = nc - d
        if lo == 0:
            head = pl.ds(0, d * CHUNK)
            acc[head, :] = states[l][head, :].astype(jnp.float32)

        if lo < min(hi, cut):
            @pl.loop(lo, min(hi, cut))
            def _(e):
                acc[span(e + d), :] = states[l][span(e + d), :].astype(jnp.float32) + product(l, e, 0)

        if max(lo, cut) < hi:
            @pl.loop(max(lo, cut), hi)
            def _(e):
                part_out[l, 0, span(e - cut), :] = product(l, e, 0).astype(jnp.bfloat16)

        if hi == nc:
            pl.when(has_next)(msg_g(l, 0).start)

    def tap_third(l, lo, hi):
        d = reach[l]
        if lo < d:
            @pl.loop(lo, min(hi, d))
            def _(e):
                part_out[l, 1, span(e), :] = product(l, e, TAPS - 1).astype(jnp.bfloat16)

            if hi >= d:
                pl.when(has_prev)(msg_g(l, 1).start)

        if max(lo, d) < hi:
            @pl.loop(max(lo, d), hi)
            def _(e):
                acc[span(e - d), :] += product(l, e, TAPS - 1)

    def neighbours(l):
        count = reach[l] * CHUNK
        for i, there, at in ((0, has_prev, 0), (1, has_next, rows - count)):
            @pl.when(there)
            def _():
                msg_g(l, i).wait_recv()
                acc[pl.ds(at, count), :] += part_in[l, i, pl.ds(0, count), :].astype(jnp.float32)

    def tap_middle(l, lo, hi):
        @pl.loop(lo, hi)
        def _(c):
            state = (acc[span(c), :] + product(l, c, 1)).astype(jnp.bfloat16)
            if l == 0:
                one[span(c), :] = state
                emit(1, c, state)
            else:
                out_ref[span(c), :] = state

    def events():
        out = []
        slots = [(l, tap) for l in range(2) for tap in ORDER]
        half = nc // 2
        for l, base in ((0, 0.0), (1, 44.0)):
            ends = {}
            for i, tap in enumerate(ORDER):
                length = 21.0 if tap == LAST else 10.5
                at = base + 10.5 * i
                for k in range(1, lines):
                    when = at + length * k / (lines - 1)
                    out.append((when, functools.partial(weights_step, l, tap, k)))
                    follows = slots.index((l, tap)) + 1
                    if k == (max(1, lines - 2) if tap == LAST else 1) and follows < len(slots):
                        out.append((when, functools.partial(weights_start, *slots[follows])))
                ends[tap] = at + length + (0.0 if tap == LAST else 5.0)
            here = [base + 1.0 + 36.8 * (e + 1) / nc for e in range(nc)]
            for e in range(nc):
                out.append((here[e], functools.partial(forward, l, e)))
                out.append((here[e] + 1.5, functools.partial(ready, l, e)))
            out.append((ends[0], functools.partial(weights_finish, l, 0)))
            out.append((ends[2], functools.partial(weights_finish, l, 2)))
            for lo in range(0, nc, 2):
                hi = min(lo + 2, nc)
                first = max(here[hi - 1] + 1.6, ends[0] + 0.1)
                third = max(here[hi - 1] + 1.7, ends[2] + 0.1)
                out.append((first, functools.partial(tap_first, l, lo, hi)))
                out.append((third, functools.partial(tap_third, l, lo, hi)))
            done = max(ends[LAST], here[-1] + 2.0) + 0.1
            out.append((done, functools.partial(neighbours, l)))
            out.append((done, functools.partial(tap_middle, l, 0, half)))
            out.append((done + 4.0, functools.partial(tap_middle, l, half, nc)))
        return [go for _, go in sorted(out, key=lambda entry: entry[0])]

    barrier = pltpu.get_barrier_semaphore()
    peers = [
        (True, y_peer, w), (True, s, x_peer), (True, s, c_peer),
        (up, s + 2, w), (down, s - 2, w), (has_next, s + 1, w), (has_prev, s - 1, w),
    ]
    expected = 3
    for there, ds, dw in peers:
        def greet(ds=ds, dw=dw):
            pl.semaphore_signal(
                barrier, inc=1, device_id=(ds, dw), device_id_type=pl.DeviceIdType.MESH
            )

        if there is True:
            greet()
        else:
            pl.when(there)(greet)
            expected = expected + there.astype(jnp.int32)
    wb[0, :, krows(z, y), :] = w1_ref[...]
    wb[1, :, krows(z, y), :] = w2_ref[...]
    pl.semaphore_wait(barrier, expected)

    weights_start(0, ORDER[0])

    @pl.loop(0, nc)
    def _(i):
        emit(0, i, x_ref[span(i), :])

    for go in events():
        go()

    for l in range(2):
        sent(l)
        weights_drain(l)
        pl.when(has_next)(msg_g(l, 0).wait_send)
        pl.when(has_prev)(msg_g(l, 1).wait_send)


def shards(n, m, x, s1, b1, w1, s2, b2, w2):
    rows, cols = x.shape
    channels = m * cols
    lines = n // 2
    dma = pltpu.SemaphoreType.DMA
    vmem = pl.BlockSpec(memory_space=pltpu.VMEM)
    return pl.pallas_call(
        functools.partial(tower_kernel, n, m),
        out_shape=jax.ShapeDtypeStruct((rows, cols), jnp.bfloat16),
        in_specs=[vmem] * 7,
        out_specs=vmem,
        scratch_shapes=[
            pltpu.VMEM((rows, channels), jnp.bfloat16),
            pltpu.VMEM((rows, channels), jnp.bfloat16),
            pltpu.VMEM((2, TAPS, channels, cols), jnp.bfloat16),
            pltpu.VMEM((rows, cols), jnp.bfloat16),
            pltpu.VMEM((rows, cols), jnp.float32),
            pltpu.VMEM((2, 2, DILATION_SECOND, cols), jnp.bfloat16),
            pltpu.VMEM((2, 2, DILATION_SECOND, cols), jnp.bfloat16),
            dma((2, 2)), dma((2, 2)),
            dma((2, 2 * TAPS, lines)), dma((2 * TAPS, lines)),
            dma((2, 2, lines)), dma((2, lines)),
            dma((2 * TAPS, lines)), dma((2 * TAPS, lines)),
        ] + [dma((2, rows // CHUNK))] * 6,
        compiler_params=pltpu.CompilerParams(
            collective_id=0, has_side_effects=True, vmem_limit_bytes=56 * 1024 * 1024
        ),
        cost_estimate=pl.CostEstimate(
            flops=4 * TAPS * rows * channels * cols,
            bytes_accessed=4 * rows * cols + 4 * TAPS * w1.shape[1] * cols,
            transcendentals=2 * rows * cols,
        ),
    )(x, s1, b1, w1, s2, b2, w2)


def solution(mesh):
    placed = (
        P("seq", "wt"),
        P("wt"),
        P("wt"),
        P(None, "seq", "wt"),
        P("wt"),
        P("wt"),
        P(None, "seq", "wt"),
    )
    n, m = mesh.shape["seq"], mesh.shape["wt"]
    return jax.shard_map(
        functools.partial(shards, n, m), mesh=mesh, in_specs=placed,
        out_specs=P("seq", "wt"), check_vma=False,
    )
```

time: 291 us -> 130 us (0.45)
  the two profiles are of different devices: /device:TPU:0 before, /device:TPU:5 now
where the time goes in v3:
time: 130 us
  Pallas kernels  127 us (98%)
  local copies, waits for them, and re-layouts  2.71 us (2%)
    pallas_call x1, Pallas kernels, shards(): pl.pallas_call(functools.partial(tower_kernel, n, m), out_shape=jax.Shape...  127 us
    unnamed x1, local copies, waits for them, and re-layouts  2.71 us

profile of v3, /device:TPU:5, one launch (start us, length us, event | category | flops | bytes accessed | tf_op | source)
XLA Modules:
  0.0 130.0 jit_solution(9550594228070330292)
XLA Ops:
  0.0 127.3 %shard_map.73 = bf16[2048,384]{1,0:T(8,128)(2,1)} custom-call(bf16[2048,384]{1,0:T(8,128)(2,1)} %x_ref.1, f32[384]{0:T(512)} %s1_ref.1, f32[384]{0:T(512)} %b1_ref.1, bf16[3,192,384]{2,1,0:T(8,128)(2,1)} %w1_ref.1, f32[384]{0:T(512)} %s2_ref.1, f32[384]{0:T(512)} %b2_ref.1, bf16[3,192,384]{2,1,0:T(8,128)(2,1)} %w2_ref.1), custom_call_target="tpu_custom_call" | custom-call | flops 14495514624 | bytes 4030464 | tf_op jit(solution)/shard_map/pallas_call | solution.py:305
  127.3 2.7 %copy.9 = bf16[2048,384]{1,0:T(8,128)(2,1)} copy(bf16[2048,384]{1,0:T(8,128)(2,1)} %shard_map.73) | data formatting | bytes 3145728

commit v4 on v3

--- a/solution.py
+++ b/solution.py
@@ -18,7 +18,7 @@
 def tower_kernel(
     n, m, x_ref, s1_ref, b1_ref, w1_ref, s2_ref, b2_ref, w2_ref, out_ref,
     hid1, hid2, wb, one, acc, part_out, part_in, s_g, r_g,
-    s_p, r_p, s_q, r_q, s_y, r_y, s_x, r_x, s_c, r_c, s_f, r_f,
+    s_p, r_p, s_y, r_y, s_x, r_x, s_c, r_c, s_f, r_f,
 ):
     s = lax.axis_index("seq")
     w = lax.axis_index("wt")
@@ -36,8 +36,6 @@
     scales = (s1_ref, s2_ref)
     shifts = (b1_ref, b2_ref)
     has_prev, has_next = s > 0, s < n - 1
-    up, down = z < lines - 1, z > 0
-    steps = ((1, up), (-1, down))
 
     def rdma(src, dst, ss, rs, ds, dw):
         return pltpu.make_async_remote_copy(
@@ -54,15 +52,16 @@
     def krows(zz, yy):
         return pl.ds(pl.multiple_of((zz * 2 + yy) * kr, kr), kr)
 
-    def msg_p(l, tap, zz, d):
-        ref = wb.at[l, tap, krows(zz, y), :]
-        i, j = (0 if d > 0 else 1), l * TAPS + tap
-        return rdma(ref, ref, s_p.at[i, j, zz], r_p.at[j, zz], s + 2 * d, w)
-
-    def msg_q(l, zz, d):
-        ref = wb.at[l, LAST, krows(zz, 1 - y), :]
-        i = 0 if d > 0 else 1
-        return rdma(ref, ref, s_q.at[i, l, zz], r_q.at[l, zz], s + 2 * d, w)
+    def others(go):
+        for k in range(1, lines):
+            for d in (1, -1):
+                zz = z + d * k
+                pl.when(jnp.logical_and(zz >= 0, zz < lines))(functools.partial(go, zz))
+
+    def msg_p(l, tap, src, dst):
+        ref = wb.at[l, tap, krows(src, y), :]
+        j = l * TAPS + tap
+        return rdma(ref, ref, s_p.at[j, dst], r_p.at[j, src], dst * 2 + y, w)
 
     def msg_y(l, tap, zz, yy):
         ref = wb.at[l, tap, krows(zz, yy), :]
@@ -70,61 +69,27 @@
         return rdma(ref, ref, s_y.at[j, zz], r_y.at[j, zz], y_peer, w)
 
     def weights_start(l, tap):
-        if tap == ORDER[1]:
-            msg_y(l, LAST, z, y).start()
-        if tap == LAST:
-            msg_y(l, LAST, z, 1 - y).wait_recv()
-        else:
-            msg_y(l, tap, z, y).start()
-        for d, there in steps:
-            @pl.when(there)
-            def _():
-                msg_p(l, tap, z, d).start()
-                if tap == LAST:
-                    msg_q(l, z, d).start()
+        msg_y(l, tap, z, y).start()
+        others(lambda zz: msg_p(l, tap, z, zz).start())
 
     def weights_step(l, tap, k):
-        for d, there in steps:
+        for d in (1, -1):
             zz = z - d * k
 
             @pl.when(jnp.logical_and(zz >= 0, zz < lines))
             def _():
-                msg_p(l, tap, zz, d).wait_recv()
-                pl.when(there)(msg_p(l, tap, zz, d).start)
-                if tap == LAST:
-                    msg_q(l, zz, d).wait_recv()
-                    pl.when(there)(msg_q(l, zz, d).start)
-                else:
-                    msg_y(l, tap, zz, y).start()
+                msg_p(l, tap, zz, z).wait_recv()
+                msg_y(l, tap, zz, y).start()
 
     def weights_finish(l, tap):
-        if tap == LAST:
-            return
         msg_y(l, tap, z, 1 - y).wait_recv()
-        for k in range(1, lines):
-            for d in (1, -1):
-                zz = z - d * k
-                pl.when(jnp.logical_and(zz >= 0, zz < lines))(
-                    msg_y(l, tap, zz, 1 - y).wait_recv
-                )
+        others(lambda zz: msg_y(l, tap, zz, 1 - y).wait_recv())
 
     def weights_drain(l):
         for tap in range(TAPS):
             msg_y(l, tap, z, y).wait_send()
-            for k in range(lines):
-                for d, there in steps:
-                    zz = z - d * k
-
-                    @pl.when(jnp.logical_and(zz >= 0, zz < lines))
-                    def _():
-                        if k and tap != LAST:
-                            msg_y(l, tap, zz, y).wait_send()
-
-                        @pl.when(there)
-                        def _():
-                            msg_p(l, tap, zz, d).wait_send()
-                            if tap == LAST:
-                                msg_q(l, zz, d).wait_send()
+            others(lambda zz: msg_y(l, tap, zz, y).wait_send())
+            others(lambda zz: msg_p(l, tap, z, zz).wait_send())
 
     def msg_x(l, e, j):
         ref = hids[l].at[span(e), lane(j)]
@@ -232,21 +197,19 @@
         for l, base in ((0, 0.0), (1, 44.0)):
             ends = {}
             for i, tap in enumerate(ORDER):
-                length = 21.0 if tap == LAST else 10.5
-                at = base + 10.5 * i
+                at = base + 14.0 * i
                 for k in range(1, lines):
-                    when = at + length * k / (lines - 1)
+                    when = at + 10.5 * k / (lines - 1)
                     out.append((when, functools.partial(weights_step, l, tap, k)))
                     follows = slots.index((l, tap)) + 1
-                    if k == (max(1, lines - 2) if tap == LAST else 1) and follows < len(slots):
+                    if k == 1 and follows < len(slots):
                         out.append((when, functools.partial(weights_start, *slots[follows])))
-                ends[tap] = at + length + (0.0 if tap == LAST else 5.0)
+                ends[tap] = at + 14.5
+                out.append((ends[tap], functools.partial(weights_finish, l, tap)))
             here = [base + 1.0 + 36.8 * (e + 1) / nc for e in range(nc)]
             for e in range(nc):
                 out.append((here[e], functools.partial(forward, l, e)))
                 out.append((here[e] + 1.5, functools.partial(ready, l, e)))
-            out.append((ends[0], functools.partial(weights_finish, l, 0)))
-            out.append((ends[2], functools.partial(weights_finish, l, 2)))
             for lo in range(0, nc, 2):
                 hi = min(lo + 2, nc)
                 first = max(here[hi - 1] + 1.6, ends[0] + 0.1)
@@ -262,8 +225,10 @@
     barrier = pltpu.get_barrier_semaphore()
     peers = [
         (True, y_peer, w), (True, s, x_peer), (True, s, c_peer),
-        (up, s + 2, w), (down, s - 2, w), (has_next, s + 1, w), (has_prev, s - 1, w),
+        (has_next, s + 1, w), (has_prev, s - 1, w),
     ]
+    for k in range(1, lines):
+        peers += [(z + k < lines, s + 2 * k, w), (z - k >= 0, s - 2 * k, w)]
     expected = 3
     for there, ds, dw in peers:
         def greet(ds=ds, dw=dw):
@@ -316,8 +281,7 @@
             pltpu.VMEM((2, 2, DILATION_SECOND, cols), jnp.bfloat16),
             pltpu.VMEM((2, 2, DILATION_SECOND, cols), jnp.bfloat16),
             dma((2, 2)), dma((2, 2)),
-            dma((2, 2 * TAPS, lines)), dma((2 * TAPS, lines)),
-            dma((2, 2, lines)), dma((2, lines)),
+            dma((2 * TAPS, lines)), dma((2 * TAPS, lines)),
             dma((2 * TAPS, lines)), dma((2 * TAPS, lines)),
         ] + [dma((2, rows // CHUNK))] * 6,
         compiler_params=pltpu.CompilerParams(

time: 130 us -> 151 us (1.16)
  the two profiles are of different devices: /device:TPU:5 before, /device:TPU:7 now
where the time goes in v4:
time: 151 us
  Pallas kernels  148 us (98%)
  local copies, waits for them, and re-layouts  2.71 us (2%)
    pallas_call x1, Pallas kernels, shards(): pl.pallas_call(functools.partial(tower_kernel, n, m), out_shape=jax.Shape...  148 us

profile of v4, /device:TPU:7, one launch (start us, length us, event | category | flops | bytes accessed | tf_op | source)
XLA Modules:
  0.0 151.0 jit_solution(3042300318537655709)
XLA Ops:
  0.0 148.3 %shard_map.73 = bf16[2048,384]{1,0:T(8,128)(2,1)} custom-call(bf16[2048,384]{1,0:T(8,128)(2,1)} %x_ref.1, f32[384]{0:T(512)} %s1_ref.1, f32[384]{0:T(512)} %b1_ref.1, bf16[3,192,384]{2,1,0:T(8,128)(2,1)} %w1_ref.1, f32[384]{0:T(512)} %s2_ref.1, f32[384]{0:T(512)} %b2_ref.1, bf16[3,192,384]{2,1,0:T(8,128)(2,1)} %w2_ref.1), custom_call_target="tpu_custom_call" | custom-call | flops 14495514624 | bytes 4030464 | tf_op jit(solution)/shard_map/pallas_call | solution.py:270
  148.3 2.7 %copy.9 = bf16[2048,384]{1,0:T(8,128)(2,1)} copy(bf16[2048,384]{1,0:T(8,128)(2,1)} %shard_map.73) | data formatting | bytes 3145728

commit v5 on v3

--- a/solution.py
+++ b/solution.py
@@ -17,7 +17,7 @@
 
 def tower_kernel(
     n, m, x_ref, s1_ref, b1_ref, w1_ref, s2_ref, b2_ref, w2_ref, out_ref,
-    hid1, hid2, wb, one, acc, part_out, part_in, s_g, r_g,
+    hid1, hid2, wb, acc, part_out, part_in, s_g, r_g,
     s_p, r_p, s_q, r_q, s_y, r_y, s_x, r_x, s_c, r_c, s_f, r_f,
 ):
     s = lax.axis_index("seq")
@@ -84,7 +84,12 @@
                     msg_q(l, z, d).start()
 
     def weights_step(l, tap, k):
-        for d, there in steps:
+        low = z < lines // 2
+        pl.when(low)(lambda: relay(l, tap, k, steps[::-1]))
+        pl.when(jnp.logical_not(low))(lambda: relay(l, tap, k, steps))
+
+    def relay(l, tap, k, ways):
+        for d, there in ways:
             zz = z - d * k
 
             @pl.when(jnp.logical_and(zz >= 0, zz < lines))
@@ -163,8 +168,6 @@
             hids[l][span(e), :], wb[l, tap], preferred_element_type=jnp.float32
         )
 
-    states = (x_ref, one)
-
     def msg_g(l, i):
         ref = pl.ds(0, reach[l] * CHUNK)
         return rdma(
@@ -175,14 +178,10 @@
     def tap_first(l, lo, hi):
         d = reach[l]
         cut = nc - d
-        if lo == 0:
-            head = pl.ds(0, d * CHUNK)
-            acc[head, :] = states[l][head, :].astype(jnp.float32)
-
         if lo < min(hi, cut):
             @pl.loop(lo, min(hi, cut))
             def _(e):
-                acc[span(e + d), :] = states[l][span(e + d), :].astype(jnp.float32) + product(l, e, 0)
+                acc[span(e + d), :] += product(l, e, 0)
 
         if max(lo, cut) < hi:
             @pl.loop(max(lo, cut), hi)
@@ -220,15 +219,21 @@
         def _(c):
             state = (acc[span(c), :] + product(l, c, 1)).astype(jnp.bfloat16)
             if l == 0:
-                one[span(c), :] = state
+                acc[span(c), :] = state.astype(jnp.float32)
                 emit(1, c, state)
             else:
                 out_ref[span(c), :] = state
 
+    last = reach[1]
+    groups = [(nc - last, nc)] + [(lo, min(lo + 2, nc - last)) for lo in range(0, nc - last, 2)]
+    place = {c: (c + last) % nc for c in range(nc)}
+
     def events():
         out = []
-        slots = [(l, tap) for l in range(2) for tap in ORDER]
-        half = nc // 2
+
+        def put(when, go, *operands):
+            out.append((when, functools.partial(go, *operands)))
+
         for l, base in ((0, 0.0), (1, 44.0)):
             ends = {}
             for i, tap in enumerate(ORDER):
@@ -236,27 +241,29 @@
                 at = base + 10.5 * i
                 for k in range(1, lines):
                     when = at + length * k / (lines - 1)
-                    out.append((when, functools.partial(weights_step, l, tap, k)))
-                    follows = slots.index((l, tap)) + 1
-                    if k == (max(1, lines - 2) if tap == LAST else 1) and follows < len(slots):
-                        out.append((when, functools.partial(weights_start, *slots[follows])))
-                ends[tap] = at + length + (0.0 if tap == LAST else 5.0)
-            here = [base + 1.0 + 36.8 * (e + 1) / nc for e in range(nc)]
-            for e in range(nc):
-                out.append((here[e], functools.partial(forward, l, e)))
-                out.append((here[e] + 1.5, functools.partial(ready, l, e)))
-            out.append((ends[0], functools.partial(weights_finish, l, 0)))
-            out.append((ends[2], functools.partial(weights_finish, l, 2)))
-            for lo in range(0, nc, 2):
-                hi = min(lo + 2, nc)
-                first = max(here[hi - 1] + 1.6, ends[0] + 0.1)
-                third = max(here[hi - 1] + 1.7, ends[2] + 0.1)
-                out.append((first, functools.partial(tap_first, l, lo, hi)))
-                out.append((third, functools.partial(tap_third, l, lo, hi)))
+                    put(when, weights_step, l, tap, k)
+                    if k == max(1, lines - 2):
+                        if i == 0:
+                            put(when, weights_start, l, LAST)
+                        if tap == LAST and l == 0:
+                            put(when, weights_start, 1, ORDER[0])
+                            put(when, weights_start, 1, ORDER[1])
+                ends[tap] = at + length + (0.0 if tap == LAST else 6.0)
+            here = [base + 1.0 + 36.8 * (i + 1) / nc for i in range(nc)]
+            for i in range(nc):
+                e = (i + nc - last) % nc
+                put(here[i], forward, l, e)
+                put(here[i] + 1.5, ready, l, e)
+            put(ends[0], weights_finish, l, 0)
+            put(ends[2], weights_finish, l, 2)
+            for lo, hi in groups:
+                come = here[place[hi - 1]]
+                put(max(come + 1.6, ends[0] + 0.1), tap_first, l, lo, hi)
+                put(max(come + 1.7, ends[2] + 0.1), tap_third, l, lo, hi)
             done = max(ends[LAST], here[-1] + 2.0) + 0.1
-            out.append((done, functools.partial(neighbours, l)))
-            out.append((done, functools.partial(tap_middle, l, 0, half)))
-            out.append((done + 4.0, functools.partial(tap_middle, l, half, nc)))
+            put(done, neighbours, l)
+            for i, (lo, hi) in enumerate(groups):
+                put(done + 4.0 * i / len(groups), tap_middle, l, lo, hi)
         return [go for _, go in sorted(out, key=lambda entry: entry[0])]
 
     barrier = pltpu.get_barrier_semaphore()
@@ -281,10 +288,14 @@
     pl.semaphore_wait(barrier, expected)
 
     weights_start(0, ORDER[0])
+    weights_start(0, ORDER[1])
 
     @pl.loop(0, nc)
     def _(i):
-        emit(0, i, x_ref[span(i), :])
+        c = lax.rem(i + nc - last, nc)
+        state = x_ref[span(c), :]
+        acc[span(c), :] = state.astype(jnp.float32)
+        emit(0, c, state)
 
     for go in events():
         go()
@@ -311,7 +322,6 @@
             pltpu.VMEM((rows, channels), jnp.bfloat16),
             pltpu.VMEM((rows, channels), jnp.bfloat16),
             pltpu.VMEM((2, TAPS, channels, cols), jnp.bfloat16),
-            pltpu.VMEM((rows, cols), jnp.bfloat16),
             pltpu.VMEM((rows, cols), jnp.float32),
             pltpu.VMEM((2, 2, DILATION_SECOND, cols), jnp.bfloat16),
             pltpu.VMEM((2, 2, DILATION_SECOND, cols), jnp.bfloat16),

time: 130 us -> 128 us (0.985)
  the two profiles are of different devices: /device:TPU:5 before, /device:TPU:0 now
where the time goes in v5:
time: 128 us
  Pallas kernels  125 us (98%)
  local copies, waits for them, and re-layouts  2.71 us (2%)
    pallas_call x1, Pallas kernels, shards(): pl.pallas_call(functools.partial(tower_kernel, n, m), out_shape=jax.Shape...  125 us
    unnamed x1, local copies, waits for them, and re-layouts  2.71 us

profile of v5, /device:TPU:0, one launch (start us, length us, event | category | flops | bytes accessed | tf_op | source)
XLA Modules:
  0.0 127.9 jit_solution(16619551234046126677)
XLA Ops:
  0.0 125.2 %shard_map.73 = bf16[2048,384]{1,0:T(8,128)(2,1)} custom-call(bf16[2048,384]{1,0:T(8,128)(2,1)} %x_ref.1, f32[384]{0:T(512)} %s1_ref.1, f32[384]{0:T(512)} %b1_ref.1, bf16[3,192,384]{2,1,0:T(8,128)(2,1)} %w1_ref.1, f32[384]{0:T(512)} %s2_ref.1, f32[384]{0:T(512)} %b2_ref.1, bf16[3,192,384]{2,1,0:T(8,128)(2,1)} %w2_ref.1), custom_call_target="tpu_custom_call" | custom-call | flops 14495514624 | bytes 4030464 | tf_op jit(solution)/shard_map/pallas_call | solution.py:316
  125.2 2.7 %copy.9 = bf16[2048,384]{1,0:T(8,128)(2,1)} copy(bf16[2048,384]{1,0:T(8,128)(2,1)} %shard_map.73) | data formatting | bytes 3145728

commit v6 on v5

--- a/solution.py
+++ b/solution.py
@@ -51,8 +51,11 @@
     def lane(j):
         return pl.ds(pl.multiple_of(j * cols, cols), cols)
 
-    def krows(zz, yy):
-        return pl.ds(pl.multiple_of((zz * 2 + yy) * kr, kr), kr)
+    def krows(zz, yy, lo=0, hi=None):
+        hi = kr if hi is None else hi
+        return pl.ds(pl.multiple_of((zz * 2 + yy) * kr + lo, 16), hi - lo)
+
+    share = (kr // 32 * 16, 0)
 
     def msg_p(l, tap, zz, d):
         ref = wb.at[l, tap, krows(zz, y), :]
@@ -60,20 +63,21 @@
         return rdma(ref, ref, s_p.at[i, j, zz], r_p.at[j, zz], s + 2 * d, w)
 
     def msg_q(l, zz, d):
-        ref = wb.at[l, LAST, krows(zz, 1 - y), :]
+        ref = wb.at[l, LAST, krows(zz, 1 - y, share[l], kr), :]
         i = 0 if d > 0 else 1
         return rdma(ref, ref, s_q.at[i, l, zz], r_q.at[l, zz], s + 2 * d, w)
 
-    def msg_y(l, tap, zz, yy):
-        ref = wb.at[l, tap, krows(zz, yy), :]
+    def msg_y(l, tap, zz, yy, whole=False):
+        part = share[l] if tap == LAST and not whole else kr
+        ref = wb.at[l, tap, krows(zz, yy, 0, part), :]
         j = l * TAPS + tap
         return rdma(ref, ref, s_y.at[j, zz], r_y.at[j, zz], y_peer, w)
 
     def weights_start(l, tap):
         if tap == ORDER[1]:
-            msg_y(l, LAST, z, y).start()
+            msg_y(l, LAST, z, y, True).start()
         if tap == LAST:
-            msg_y(l, LAST, z, 1 - y).wait_recv()
+            msg_y(l, LAST, z, 1 - y, True).wait_recv()
         else:
             msg_y(l, tap, z, y).start()
         for d, there in steps:
@@ -99,13 +103,14 @@
                 if tap == LAST:
                     msg_q(l, zz, d).wait_recv()
                     pl.when(there)(msg_q(l, zz, d).start)
-                else:
+                if tap != LAST or share[l]:
                     msg_y(l, tap, zz, y).start()
 
     def weights_finish(l, tap):
-        if tap == LAST:
+        if tap == LAST and not share[l]:
             return
-        msg_y(l, tap, z, 1 - y).wait_recv()
+        if tap != LAST:
+            msg_y(l, tap, z, 1 - y).wait_recv()
         for k in range(1, lines):
             for d in (1, -1):
                 zz = z - d * k
@@ -115,14 +120,14 @@
 
     def weights_drain(l):
         for tap in range(TAPS):
-            msg_y(l, tap, z, y).wait_send()
+            msg_y(l, tap, z, y, True).wait_send()
             for k in range(lines):
                 for d, there in steps:
                     zz = z - d * k
 
                     @pl.when(jnp.logical_and(zz >= 0, zz < lines))
                     def _():
-                        if k and tap != LAST:
+                        if k and (tap != LAST or share[l]):
                             msg_y(l, tap, zz, y).wait_send()
 
                         @pl.when(there)
@@ -261,6 +266,7 @@
                 put(max(come + 1.6, ends[0] + 0.1), tap_first, l, lo, hi)
                 put(max(come + 1.7, ends[2] + 0.1), tap_third, l, lo, hi)
             done = max(ends[LAST], here[-1] + 2.0) + 0.1
+            put(done, weights_finish, l, LAST)
             put(done, neighbours, l)
             for i, (lo, hi) in enumerate(groups):
                 put(done + 4.0 * i / len(groups), tap_middle, l, lo, hi)

time: 128 us -> 125 us (0.977)
  Pallas kernels: 125 us -> 122 us
    pallas_call x1, Pallas kernels: 125 us -> 122 us  [shards(): pl.pallas_call(functools.partial(tower_kernel, n, m), out_shape=jax.Shape...]
where the time goes in v6:
time: 125 us
  Pallas kernels  122 us (98%)
  local copies, waits for them, and re-layouts  2.71 us (2%)
    pallas_call x1, Pallas kernels, shards(): pl.pallas_call(functools.partial(tower_kernel, n, m), out_shape=jax.Shape...  122 us
    unnamed x1, local copies, waits for them, and re-layouts  2.71 us

profile of v6, /device:TPU:0, one launch (start us, length us, event | category | flops | bytes accessed | tf_op | source)
XLA Modules:
  0.0 124.9 jit_solution(15994423682508564948)
XLA Ops:
  0.0 122.2 %shard_map.73 = bf16[2048,384]{1,0:T(8,128)(2,1)} custom-call(bf16[2048,384]{1,0:T(8,128)(2,1)} %x_ref.1, f32[384]{0:T(512)} %s1_ref.1, f32[384]{0:T(512)} %b1_ref.1, bf16[3,192,384]{2,1,0:T(8,128)(2,1)} %w1_ref.1, f32[384]{0:T(512)} %s2_ref.1, f32[384]{0:T(512)} %b2_ref.1, bf16[3,192,384]{2,1,0:T(8,128)(2,1)} %w2_ref.1), custom_call_target="tpu_custom_call" | custom-call | flops 14495514624 | bytes 4030464 | tf_op jit(solution)/shard_map/pallas_call | solution.py:322
  122.2 2.7 %copy.9 = bf16[2048,384]{1,0:T(8,128)(2,1)} copy(bf16[2048,384]{1,0:T(8,128)(2,1)} %shard_map.73) | data formatting | bytes 3145728

commit v7 on v6

--- a/solution.py
+++ b/solution.py
@@ -55,7 +55,7 @@
         hi = kr if hi is None else hi
         return pl.ds(pl.multiple_of((zz * 2 + yy) * kr + lo, 16), hi - lo)
 
-    share = (kr // 32 * 16, 0)
+    share = (kr // 32 * 16, kr // 32 * 16)
 
     def msg_p(l, tap, zz, d):
         ref = wb.at[l, tap, krows(zz, y), :]

time: 125 us -> 130 us (1.040)
  Pallas kernels: 122 us -> 128 us
    pallas_call x1, Pallas kernels: 122 us -> 128 us  [shards(): pl.pallas_call(functools.partial(tower_kernel, n, m), out_shape=jax.Shape...]
where the time goes in v7:
time: 130 us
  Pallas kernels  128 us (98%)
  local copies, waits for them, and re-layouts  2.71 us (2%)
    pallas_call x1, Pallas kernels, shards(): pl.pallas_call(functools.partial(tower_kernel, n, m), out_shape=jax.Shape...  128 us
    unnamed x1, local copies, waits for them, and re-layouts  2.71 us

profile of v7, /device:TPU:0, one launch (start us, length us, event | category | flops | bytes accessed | tf_op | source)
XLA Modules:
  0.0 130.3 jit_solution(14719042891290904007)
XLA Ops:
  0.0 127.6 %shard_map.73 = bf16[2048,384]{1,0:T(8,128)(2,1)} custom-call(bf16[2048,384]{1,0:T(8,128)(2,1)} %x_ref.1, f32[384]{0:T(512)} %s1_ref.1, f32[384]{0:T(512)} %b1_ref.1, bf16[3,192,384]{2,1,0:T(8,128)(2,1)} %w1_ref.1, f32[384]{0:T(512)} %s2_ref.1, f32[384]{0:T(512)} %b2_ref.1, bf16[3,192,384]{2,1,0:T(8,128)(2,1)} %w2_ref.1), custom_call_target="tpu_custom_call" | custom-call | flops 14495514624 | bytes 4030464 | tf_op jit(solution)/shard_map/pallas_call | solution.py:322
  127.6 2.7 %copy.9 = bf16[2048,384]{1,0:T(8,128)(2,1)} copy(bf16[2048,384]{1,0:T(8,128)(2,1)} %shard_map.73) | data formatting | bytes 3145728
